TPU v7x, 128 devices: a whole 4x4x4 slice. The times are simulated.
128 devices in a mesh: section: 16 (over x_lo, z, core), seq: 8 (over y, x_hi).
Axes of the slice: x: 4 (x_hi: 2, x_lo: 2; x = x_hi * 2 + x_lo), y: 4, z: 4, core: 2. Of those that a mesh axis runs over, the one named last changes fastest.
Arguments:
- queries: bfloat16 [16, 1024, 8192], P('section', 'seq'), may hold values from -48 to 48
- key_states: bfloat16 [16, 1024, 1024], P('section', 'seq'), may hold values from -6 to 6
- section_value_states: bfloat16 [16, 1024, 1024], P('section', 'seq'), may hold values from -6 to 6
- out_grad: bfloat16 [16, 1024, 8192], P('section', 'seq'), may hold values from -1.5 to 1.5
- layer_input: bfloat16 [16, 1024, 8192], P('section', 'seq'), may hold values from -6 to 6
- doc_segments: int32 [16, 1024], P('section', 'seq'), may hold values from 0 to 3, never falling along the last dimension, each value on 1 to 512 neighbouring positions
Outputs:
- query_grad: bfloat16 [16, 1024, 8192], P('section', 'seq')
- key_grad: bfloat16 [16, 1024, 1024], P('section', 'seq')
- weight_grad: bfloat16 [16, 8192, 1024], P('section', None, 'seq')
Inputs may be any that keep to these rules, and one draw needn't show every extreme that they name: `doc_segments`: document numbers never fall along a section's positions; a document holds at most 512 positions.
All inputs are finite; a program needn't handle non-finite values.
Results may differ from a plain program's by a relative error of at most 0.012.
The roundings to bfloat16 on the way count: a program that leaves them out, or rounds other values in their place, can miss the bound.
Values may be sent and summed in bfloat16 or wider, within the bound.
A program may use at most 128 MiB of HBM per device.

v0:
```python
import math

import jax
import jax.numpy as jnp
from jax import lax
from jax.sharding import PartitionSpec as P

HEAD_WIDTH = 128


def group_pass(query_group, key_col, value_col, grad_group, allowed):
    scale_factor = 1.0 / math.sqrt(key_col.shape[1])

    def one_head(totals, head_inputs):
        query_one, grad_one = head_inputs
        key_acc, value_acc = totals
        scores = jnp.dot(query_one, key_col.T, preferred_element_type=jnp.float32) * scale_factor
        scores = jnp.where(allowed, scores, -jnp.inf)
        row_max = jnp.max(scores, axis=1, keepdims=True)
        weights = jnp.exp(scores - row_max)
        attention = weights / jnp.sum(weights, axis=1, keepdims=True)
        probs_low = attention.astype(jnp.bfloat16)
        attended = jnp.dot(probs_low, value_col, preferred_element_type=jnp.float32).astype(
            jnp.bfloat16
        )
        attended = lax.optimization_barrier(attended)
        row_delta = jnp.sum(
            grad_one.astype(jnp.float32) * attended.astype(jnp.float32), axis=1, keepdims=True
        )
        dprobs = jnp.dot(grad_one, value_col.T, preferred_element_type=jnp.float32)
        dscores = (attention * (dprobs - row_delta) * scale_factor).astype(jnp.bfloat16)
        query_part = jnp.dot(dscores, key_col, preferred_element_type=jnp.float32).astype(
            jnp.bfloat16
        )
        key_acc = key_acc + jnp.dot(dscores.T, query_one, preferred_element_type=jnp.float32)
        value_acc = value_acc + jnp.dot(probs_low.T, grad_one, preferred_element_type=jnp.float32)
        return ((key_acc, value_acc), query_part)

    starting = jnp.zeros(key_col.shape, jnp.float32)
    (key_acc, value_acc), query_parts = lax.scan(
        one_head, (starting, starting), (query_group, grad_group)
    )
    return (query_parts, key_acc.astype(jnp.bfloat16), value_acc.astype(jnp.bfloat16))


def attention_grads(query_cols, key_cols, value_cols, grad_cols, doc_ids):
    length = query_cols.shape[0]
    kv_heads = key_cols.shape[1] // HEAD_WIDTH
    q_heads = query_cols.shape[1] // HEAD_WIDTH
    group_size = q_heads // kv_heads
    position = jnp.arange(length, dtype=jnp.int32)
    allowed = (position[:, None] >= position[None, :]) & (doc_ids[:, None] == doc_ids[None, :])
    query_split = query_cols.reshape(length, kv_heads, group_size, HEAD_WIDTH).transpose(1, 2, 0, 3)
    grad_split = grad_cols.reshape(length, kv_heads, group_size, HEAD_WIDTH).transpose(1, 2, 0, 3)
    key_split = key_cols.reshape(length, kv_heads, HEAD_WIDTH).transpose(1, 0, 2)
    value_split = value_cols.reshape(length, kv_heads, HEAD_WIDTH).transpose(1, 0, 2)

    def per_group(inputs):
        return group_pass(inputs[0], inputs[1], inputs[2], inputs[3], allowed)

    query_parts, key_parts, value_parts = lax.map(
        per_group, (query_split, key_split, value_split, grad_split)
    )
    query_out = query_parts.transpose(2, 0, 1, 3).reshape(length, q_heads * HEAD_WIDTH)
    key_out = key_parts.transpose(1, 0, 2).reshape(length, kv_heads * HEAD_WIDTH)
    value_out = value_parts.transpose(1, 0, 2).reshape(length, kv_heads * HEAD_WIDTH)
    return (query_out, key_out, value_out)


def row_product(shard_rows, value_rows):
    return lax.dot_general(
        shard_rows, value_rows, (((0,), (0,)), ((), ())), preferred_element_type=jnp.float32
    )


def local(queries, key_states, section_value_states, out_grad, layer_input, doc_segments):
    query_head, key_head, value_head, grad_head = (
        lax.all_to_all(queries[0], "seq", split_axis=1, concat_axis=0, tiled=True),
        lax.all_to_all(key_states[0], "seq", split_axis=1, concat_axis=0, tiled=True),
        lax.all_to_all(section_value_states[0], "seq", split_axis=1, concat_axis=0, tiled=True),
        lax.all_to_all(out_grad[0], "seq", split_axis=1, concat_axis=0, tiled=True),
    )
    doc_ids = lax.all_gather(doc_segments[0], "seq", axis=0, tiled=True)
    query_out, key_out, value_out = attention_grads(
        query_head, key_head, value_head, grad_head, doc_ids
    )
    query_back, key_back = (
        lax.all_to_all(query_out, "seq", split_axis=0, concat_axis=1, tiled=True),
        lax.all_to_all(key_out, "seq", split_axis=0, concat_axis=1, tiled=True),
    )
    section_count = lax.axis_size("section")
    section_grad = row_product(lax.all_gather(layer_input[0], "seq", axis=0, tiled=True), value_out)
    width_rows = section_grad.shape[0]
    pieces = section_grad.reshape(section_count, width_rows // section_count, section_grad.shape[1])
    received = lax.all_to_all(pieces, "section", split_axis=0, concat_axis=0, tiled=True)
    summed = received + received[::-1]
    returned = lax.all_to_all(
        summed.astype(jnp.bfloat16), "section", split_axis=0, concat_axis=0, tiled=True
    ).astype(summed.dtype)
    paired = returned.reshape(section_grad.shape)
    return (query_back[None], key_back[None], paired.astype(jnp.bfloat16)[None])


def solution(mesh):
    in_specs = (
        P("section", "seq", None),
        P("section", "seq", None),
        P("section", "seq", None),
        P("section", "seq", None),
        P("section", "seq", None),
        P("section", "seq"),
    )
    out_specs = (P("section", "seq", None), P("section", "seq", None), P("section", None, "seq"))
    return jax.shard_map(local, mesh=mesh, in_specs=in_specs, out_specs=out_specs, check_vma=False)
```

profile of v0, /device:TPU:1, one launch (start us, length us, event | category | flops | bytes accessed | tf_op | source)
XLA Modules:
  0.0 416.5 jit_solution(9854583054386464406)
XLA Ops:
  8.9 7.5 %all-to-all-start.1 = ((bf16[128,8,128]{2,0,1:T(8,128)(2,1)}), bf16[128,8,128]{2,0,1:T(8,128)(2,1)S(1)}, u32[]{:S(2)}, u32[]{:S(2)}) async-start(bf16[128,8,128]{2,0,1:T(8,128)(2,1)} %copy.49), calls=%async_computation.1 | async-start | bytes 524288 | tf_op jit(solution)/shard_map/all_to_all | solution.py:79
  16.4 3.0 copy.63
  19.4 2.5 copy.48
  21.9 2.2 all-to-all-done.1
  24.0 4.5 %all-to-all-start = ((bf16[128,8,1024]{2,0,1:T(8,128)(2,1)}), bf16[128,8,1024]{2,0,1:T(8,128)(2,1)S(1)}, u32[]{:S(2)}, u32[]{:S(2)}) async-start(bf16[128,8,1024]{2,0,1:T(8,128)(2,1)} %copy.48), calls=%async_computation | async-start | bytes 4194304 | tf_op jit(solution)/shard_map/all_to_all | solution.py:78
  29.3 3.0 copy.66
  32.3 2.5 copy.50
  34.7 22.6 %all-to-all-done = bf16[128,8,1024]{2,0,1:T(8,128)(2,1)S(1)} async-done(((bf16[128,8,1024]{2,0,1:T(8,128)(2,1)}), bf16[128,8,1024]{2,0,1:T(8,128)(2,1)S(1)}, u32[]{:S(2)}, u32[]{:S(2)}) %all-to-all-start) | async-done | bytes 2097184 | tf_op jit(solution)/shard_map/all_to_all | solution.py:78
  57.4 5.3 %all-to-all-start.2 = ((bf16[128,8,1024]{2,0,1:T(8,128)(2,1)}), bf16[128,8,1024]{2,0,1:T(8,128)(2,1)}, u32[]{:S(2)}, u32[]{:S(2)}) async-start(bf16[128,8,1024]{2,0,1:T(8,128)(2,1)} %copy.50), calls=%async_computation.2 | async-start | bytes 4194304 | tf_op jit(solution)/shard_map/all_to_all | solution.py:81
  63.5 37.1 %all-to-all-done.2 = bf16[128,8,1024]{2,0,1:T(8,128)(2,1)} async-done(((bf16[128,8,1024]{2,0,1:T(8,128)(2,1)}), bf16[128,8,1024]{2,0,1:T(8,128)(2,1)}, u32[]{:S(2)}, u32[]{:S(2)}) %all-to-all-start.2) | async-done | bytes 2097184 | tf_op jit(solution)/shard_map/all_to_all | solution.py:81
  100.6 3.4 all-to-all-start.3
  104.0 19.7 %all-gather = s32[1,1024]{1,0:T(1,128)S(1)} all-gather(s32[1,128]{1,0:T(1,128)S(1)} %copy-done.6), channel_id=2, replica_groups=mesh['section'=16,'seq'=8] {'seq'}, dimensions={1}, use_global_device_ids=true | all-gather | bytes 4608 | tf_op jit(solution)/shard_map/all_gather | solution.py:83
  124.6 2.4 copy.67
  128.7 116.7 %while.26 = (s32[]{:T(128)}, f32[1024,128]{1,0:T(8,128)S(1)}, f32[1024,128]{1,0:T(8,128)S(1)}, bf16[8,1024,128]{2,1,0:T(8,128)(2,1)}, bf16[8,1024,128]{2,1,0:T(8...) while((s32[]{:T(128)}, f32[1024,128]{1,0:T(8,128)S(1)}, ...), condition=%wide.region_4.5_spmd.clone, body=%wide.region_0.4_spmd.clone.sunk | while | flops 1629746176 | bytes 60862724 | solution.py:40
  134.0 3.4 multiply_convert_fusion.2
  137.4 2.4 convolution_add_fusion.4
  148.5 3.4 multiply_convert_fusion.2
  151.9 2.4 convolution_add_fusion.4
  163.1 3.4 multiply_convert_fusion.2
  166.5 2.4 convolution_add_fusion.4
  172.5 2.0 fusion.59
  177.7 3.4 multiply_convert_fusion.2
  181.1 2.4 convolution_add_fusion.4
  187.1 2.0 fusion.59
  192.3 3.4 multiply_convert_fusion.2
  195.7 2.4 convolution_add_fusion.4
  206.9 3.4 multiply_convert_fusion.2
  210.3 2.4 convolution_add_fusion.4
  216.2 2.0 fusion.59
  221.5 3.4 multiply_convert_fusion.2
  224.9 2.4 convolution_add_fusion.4
  236.1 3.4 multiply_convert_fusion.2
  239.5 2.4 convolution_add_fusion.4
  246.1 3.4 all-to-all-start.5
  249.6 8.5 %fusion.20 = f32[128,8192]{1,0:T(8,128)S(1)} fusion(bf16[1,1024,8192]{2,1,0:T(8,128)(2,1)} %all-gather.4.cloned.1.call-done, f32[1024,128]{1,0:T(8,128)S(1)} %get-tuple-element.81), kind=kOutput, calls=%fused_computation.28 | convolution fusion | flops 2147614720 | bytes 21495808 | tf_op jit(solution)/shard_map/dot_general | solution.py:71
  258.1 2.5 copy.70
  260.6 14.0 %all-to-all-start.6 = ((f32[16,512,128]{1,2,0:T(8,128)}), f32[16,512,128]{1,2,0:T(8,128)}, u32[]{:S(2)}, u32[]{:S(2)}) async-start(f32[16,512,128]{1,2,0:T(8,128)} %bitcast.114), calls=%async_computation.6 | async-start | bytes 8388608 | tf_op jit(solution)/shard_map/all_to_all | solution.py:95
  274.5 2.9 copy.54
  277.5 2.3 all_to_all.90
  279.8 50.4 %all-to-all-done.6 = f32[16,512,128]{1,2,0:T(8,128)} async-done(((f32[16,512,128]{1,2,0:T(8,128)}), f32[16,512,128]{1,2,0:T(8,128)}, u32[]{:S(2)}, u32[]{:S(2)}) %all-to-all-start.6) | async-done | bytes 4194336 | tf_op jit(solution)/shard_map/all_to_all | solution.py:95
  330.2 7.4 %all-to-all-start.4 = ((bf16[8,128,1024]{2,1,0:T(8,128)(2,1)}), bf16[8,128,1024]{2,1,0:T(8,128)(2,1)S(1)}, u32[]{:S(2)}, u32[]{:S(2)}) async-start(bf16[8,128,1024]{2,1,0:T(8,128)(2,1)} %all_to_all.90), calls=%async_computation.4 | async-start | bytes 4194304 | tf_op jit(solution)/shard_map/all_to_all | solution.py:88
  337.6 5.6 %fusion.22 = bf16[16,512,128]{1,2,0:T(8,128)(2,1)} fusion(f32[16,512,128]{1,2,0:T(8,128)} %all-to-all-done.6), kind=kLoop, calls=%fused_computation.31 | loop fusion | flops 2097152 | bytes 6291456 | tf_op jit(solution)/shard_map/convert_element_type | solution.py:98
  343.2 21.9 %all-to-all-done.4 = bf16[8,128,1024]{2,1,0:T(8,128)(2,1)S(1)} async-done(((bf16[8,128,1024]{2,1,0:T(8,128)(2,1)}), bf16[8,128,1024]{2,1,0:T(8,128)(2,1)S(1)}, u32[]{:S(2)}, u32[]{:S(2)}) %all-to-all-start.4) | async-done | bytes 2097184 | tf_op jit(solution)/shard_map/all_to_all | solution.py:88
  365.1 12.5 %all-to-all-start.7 = ((bf16[16,512,128]{1,2,0:T(8,128)(2,1)}), bf16[16,512,128]{1,2,0:T(8,128)(2,1)}, u32[]{:S(2)}, u32[]{:S(2)}) async-start(bf16[16,512,128]{1,2,0:T(8,128)(2,1)} %fusion.22), calls=%async_computation.7 | async-start | bytes 4194304 | tf_op jit(solution)/shard_map/all_to_all | solution.py:97
  378.7 2.4 copy.55
  381.1 4.1 copy.59
  385.1 20.6 %all-to-all-done.7 = bf16[16,512,128]{1,2,0:T(8,128)(2,1)} async-done(((bf16[16,512,128]{1,2,0:T(8,128)(2,1)}), bf16[16,512,128]{1,2,0:T(8,128)(2,1)}, u32[]{:S(2)}, u32[]{:S(2)}) %all-to-all-start.7) | async-done | bytes 2097184 | tf_op jit(solution)/shard_map/all_to_all | solution.py:97
  405.8 3.9 copy.58
  (141 shorter events, 71.4 us)
Async XLA Ops:
  8.9 15.1 %all-to-all-start.1 = ((bf16[128,8,128]{2,0,1:T(8,128)(2,1)}), bf16[128,8,128]{2,0,1:T(8,128)(2,1)S(1)}, u32[]{:S(2)}, u32[]{:S(2)}) async-start(bf16[128,8,128]{2,0,1:T(8,128)(2,1)} %copy.49), calls=%async_computation.1 | async-start | bytes 524288 | tf_op jit(solution)/shard_map/all_to_all | solution.py:79
  24.0 5.2 %copy-start.4 = (bf16[128,8,128]{2,0,1:T(8,128)(2,1)}, bf16[128,8,128]{2,0,1:T(8,128)(2,1)S(1)}, u32[]{:S(2)}) copy-start(bf16[128,8,128]{2,0,1:T(8,128)(2,1)S(1)} %all-to-all-done.1) | copy-start | bytes 786436
  24.0 33.3 %all-to-all-start = ((bf16[128,8,1024]{2,0,1:T(8,128)(2,1)}), bf16[128,8,1024]{2,0,1:T(8,128)(2,1)S(1)}, u32[]{:S(2)}, u32[]{:S(2)}) async-start(bf16[128,8,1024]{2,0,1:T(8,128)(2,1)} %copy.48), calls=%async_computation | async-start | bytes 4194304 | tf_op jit(solution)/shard_map/all_to_all | solution.py:78
  28.5 221.0 %all-gather.4.cloned.1.call-start = ((), (), s32[]{:S(2)}) async-start(), calls=%async_computation.8 | async-start | bytes 18874368 | tf_op jit(solution)/shard_map/all_gather | solution.py:92
  34.7 27.9 %copy-start.3 = (bf16[1,128,1024]{2,1,0:T(8,128)(2,1)S(1)}, bf16[1,128,1024]{2,1,0:T(8,128)(2,1)}, u32[]{:S(2)}) copy-start(bf16[1,128,1024]{2,1,0:T(8,128)(2,1)} %param.10) | copy-start | bytes 786436
  34.7 69.3 %copy-start.6 = (s32[1,128]{1,0:T(1,128)S(1)}, s32[1,128]{1,0:T(1,128)}, u32[]{:S(2)}) copy-start(s32[1,128]{1,0:T(1,128)} %param.13) | copy-start | bytes 1540
  57.4 43.2 %all-to-all-start.2 = ((bf16[128,8,1024]{2,0,1:T(8,128)(2,1)}), bf16[128,8,1024]{2,0,1:T(8,128)(2,1)}, u32[]{:S(2)}, u32[]{:S(2)}) async-start(bf16[128,8,1024]{2,0,1:T(8,128)(2,1)} %copy.50), calls=%async_computation.2 | async-start | bytes 4194304 | tf_op jit(solution)/shard_map/all_to_all | solution.py:81
  100.6 28.2 %all-to-all-start.3 = ((bf16[128,8,128]{2,0,1:T(8,128)(2,1)}), bf16[128,8,128]{2,0,1:T(8,128)(2,1)S(1)}, u32[]{:S(2)}, u32[]{:S(2)}) async-start(bf16[128,8,128]{2,0,1:T(8,128)(2,1)} %copy.51), calls=%async_computation.3 | async-start | bytes 524288 | tf_op jit(solution)/shard_map/all_to_all | solution.py:80
  128.7 2.0 copy-start.1
  139.8 1.9 copy-start
  139.8 1.9 copy-start.5
  141.7 1.6 copy-start.2
  143.3 2.0 copy-start.1
  154.3 1.9 copy-start
  154.3 1.9 copy-start.5
  156.3 1.6 copy-start.2
  157.9 2.0 copy-start.1
  168.9 1.9 copy-start
  168.9 1.9 copy-start.5
  170.8 1.6 copy-start.2
  172.5 2.0 copy-start.1
  183.5 1.9 copy-start
  183.5 1.9 copy-start.5
  185.5 1.6 copy-start.2
  187.1 2.0 copy-start.1
  198.1 1.9 copy-start
  198.1 1.9 copy-start.5
  200.1 1.6 copy-start.2
  201.7 2.0 copy-start.1
  212.7 1.9 copy-start
  212.7 1.9 copy-start.5
  214.6 1.6 copy-start.2
  216.2 2.0 copy-start.1
  227.3 1.9 copy-start
  227.3 1.9 copy-start.5
  229.2 1.6 copy-start.2
  230.8 2.0 copy-start.1
  241.9 1.9 copy-start
  241.9 1.9 copy-start.5
  243.8 1.6 copy-start.2
  246.1 14.4 %all-to-all-start.5 = ((bf16[8,128,128]{2,1,0:T(8,128)(2,1)}), bf16[8,128,128]{2,1,0:T(8,128)(2,1)S(1)}, u32[]{:S(2)}, u32[]{:S(2)}) async-start(bf16[8,128,128]{2,1,0:T(8,128)(2,1)} %bitcast.15), calls=%async_computation.5 | async-start | bytes 524288 | tf_op jit(solution)/shard_map/all_to_all | solution.py:89
  260.6 69.6 %all-to-all-start.6 = ((f32[16,512,128]{1,2,0:T(8,128)}), f32[16,512,128]{1,2,0:T(8,128)}, u32[]{:S(2)}, u32[]{:S(2)}) async-start(f32[16,512,128]{1,2,0:T(8,128)} %bitcast.114), calls=%async_computation.6 | async-start | bytes 8388608 | tf_op jit(solution)/shard_map/all_to_all | solution.py:95
  330.2 34.9 %all-to-all-start.4 = ((bf16[8,128,1024]{2,1,0:T(8,128)(2,1)}), bf16[8,128,1024]{2,1,0:T(8,128)(2,1)S(1)}, u32[]{:S(2)}, u32[]{:S(2)}) async-start(bf16[8,128,1024]{2,1,0:T(8,128)(2,1)} %all_to_all.90), calls=%async_computation.4 | async-start | bytes 4194304 | tf_op jit(solution)/shard_map/all_to_all | solution.py:88
  365.1 40.6 %all-to-all-start.7 = ((bf16[16,512,128]{1,2,0:T(8,128)(2,1)}), bf16[16,512,128]{1,2,0:T(8,128)(2,1)}, u32[]{:S(2)}, u32[]{:S(2)}) async-start(bf16[16,512,128]{1,2,0:T(8,128)(2,1)} %fusion.22), calls=%async_computation.7 | async-start | bytes 4194304 | tf_op jit(solution)/shard_map/all_to_all | solution.py:97
Sparse Core Ops, SparseCore 0:
  31.7 210.1 all-gather.3
where the time goes:
time: 419 us; the launch traced here: 417 us
  waiting for transfers between devices  156 us (37%)
  matrix products  104 us (25%)
  starting transfers between devices  58 us (14%)
  local copies, waits for them, and re-layouts  38.6 us (9%)
  other arithmetic  26.2 us (6%)
  blocking collectives  19.7 us (5%)
  between operations  14.2 us (3%)
    all_to_all x1, waiting for transfers between devices, local(): lax.all_to_all(pieces, 'section', split_axis=0, concat_axis=0, tiled=True)  50.4 us
    all_to_all x1, waiting for transfers between devices, local(): lax.all_to_all(out_grad[0], 'seq', split_axis=1, concat_axis=0, tiled=True)  37.1 us
    dot_general x8, matrix products, one_head(): dprobs = jnp.dot(grad_one, value_col.T, preferred_element_type=jnp.float32)  27.2 us
    all_to_all x1, waiting for transfers between devices, local(): lax.all_to_all(queries[0], 'seq', split_axis=1, concat_axis=0, tiled=True)  22.6 us
    all_to_all x1, waiting for transfers between devices, local(): lax.all_to_all(query_out, 'seq', split_axis=0, concat_axis=1, tiled=True)  21.9 us
    all_to_all x1, waiting for transfers between devices, local(): lax.all_to_all(summed.astype(jnp.bfloat16), 'section', split_axis=0, conc...  20.6 us
    all_gather x1, blocking collectives, local(): doc_ids = lax.all_gather(doc_segments[0], 'seq', axis=0, tiled=True)  19.7 us
    dot_general x8, matrix products, one_head(): jnp.dot(dscores.T, query_one, preferred_element_type=jnp.float32)  19 us
  transfers between devices with their start and end apart: 9, of which 6 were waited for; matrix products, arithmetic and copies ran while one was open for 38% of the time, Pallas kernels for 0%

commit v1 on v0

v1 whole, which is shorter than its diff:
```python
import math

import jax
import jax.numpy as jnp
from jax import lax
from jax.experimental import pallas as pl
from jax.experimental.pallas import tpu as pltpu
from jax.sharding import PartitionSpec as P

MESH = pl.DeviceIdType.MESH
W = 128
G = 8
REP = 8
NSLOT = 5
NB = 4
GB = G // NB
ROWS = 512
SCALE = 1.0 / math.sqrt(W)
LOG2E = 1.4426950408889634
BF = jnp.bfloat16
F32 = jnp.float32


def dot(a, b, ca, cb):
    return lax.dot_general(a, b, (((ca,), (cb,)), ((), ())), preferred_element_type=F32)


def kernel(
    q_hbm, k_ref, v_ref, do_hbm, l_hbm, doc_ref,
    dq_hbm, dk_hbm, wg_hbm,
    q_vm, do_vm, kvx, docx, bias, tx, rx, own, dvall, lall, wout, dq_vm, dk_vm, pl_vm, ds_vm,
    in_sem, kv_ss, kv_rs, doc_ss, doc_rs, l_ss, l_rs, p_ss, p_rs, x1_ss, x1_rs, x2_ss, x2_rs,
    o_ss, o_rs, out_sem,
):
    s = lax.axis_index("section")
    j = lax.axis_index("seq")
    sec = s // 8
    s0 = s + sec * (15 - 2 * s)
    me = sec * 8 + j
    y = j // 2
    xh = j % 2

    def dev(sec2, j2):
        return (s0 + sec2 * (15 - 2 * s0), j2)

    def remote(src, dst, ss, rs, to):
        return pltpu.make_async_remote_copy(
            src_ref=src, dst_ref=dst, send_sem=ss, recv_sem=rs, device_id=to, device_id_type=MESH
        )

    q_in = pltpu.make_async_copy(q_hbm, q_vm, in_sem.at[0])
    do_in = pltpu.make_async_copy(do_hbm, do_vm, in_sem.at[1])
    q_in.start()
    do_in.start()
    l_own = pltpu.make_async_copy(
        l_hbm.at[:, pl.ds(pl.multiple_of(me * ROWS, ROWS), ROWS)], lall.at[sec, j], in_sem.at[2]
    )
    l_own.start()

    barrier = pltpu.get_barrier_semaphore()

    def greet(k, c):
        r = (me + k) % 16
        pl.semaphore_signal(barrier, inc=1, device_id=dev(r // 8, r % 8), device_id_type=MESH)
        return c

    lax.fori_loop(1, 16, greet, 0)

    for g in range(G):
        kvx[g, 0, 0] = k_ref[:, g * W:(g + 1) * W]
        kvx[g, 1, 0] = v_ref[:, g * W:(g + 1) * W]
    docx[0] = jnp.broadcast_to(doc_ref[...], (8, W))
    for d in range(1, NSLOT):
        @pl.when(j < d)
        def _():
            kvx[:, :, d] = jnp.zeros((G, 2, W, W), BF)
            docx[d] = jnp.zeros((8, W), jnp.int32)

    pl.semaphore_wait(barrier, 15)

    def kv_copy(b, d):
        hs = pl.ds(b * GB, GB)
        return remote(
            kvx.at[hs, :, 0], kvx.at[hs, :, d], kv_ss.at[b, d], kv_rs.at[b, d], (s, j + d)
        )

    def doc_copy(d):
        return remote(docx.at[0], docx.at[d], doc_ss.at[d], doc_rs.at[d], (s, j + d))

    for d in range(1, NSLOT):
        @pl.when(j + d < 8)
        def _():
            doc_copy(d).start()

    def send_kv(b, c):
        for d in range(1, NSLOT):
            @pl.when(j + d < 8)
            def _():
                kv_copy(b, d).start()
        return c

    lax.fori_loop(0, NB, send_kv, 0)

    def l_copy(k):
        r = (me + k) % 16
        return remote(
            l_hbm.at[:, pl.ds(pl.multiple_of(r * ROWS, ROWS), ROWS)], lall.at[sec, j],
            l_ss.at[k], l_rs.at[k], dev(r // 8, r % 8),
        )

    def send_l(k, c):
        l_copy(k).start()
        return c

    lax.fori_loop(1, 16, send_l, 0)

    for d in range(1, NSLOT):
        @pl.when(j >= d)
        def _():
            doc_copy(d).wait_recv()

    row = lax.broadcasted_iota(jnp.int32, (W, W), 0)
    col = lax.broadcasted_iota(jnp.int32, (W, W), 1)
    q_doc = jnp.broadcast_to(docx[0, 0:1], (W, W)).astype(F32)
    for d in range(NSLOT):
        key_doc = jnp.broadcast_to(docx[d, 0:1], (W, W)).astype(F32).T
        seen = (key_doc == q_doc) & (j >= d)
        if d == 0:
            seen = seen & (row <= col)
        bias[d * W:(d + 1) * W] = jnp.where(seen, 0.0, -jnp.inf).astype(F32)

    q_in.wait()
    do_in.wait()

    def attention(b, g):
        keys = kvx.at[g, 0]
        values = kvx.at[g, 1]

        def pair(p, c):
            at = pl.multiple_of((g * REP + 2 * p) * W, 2 * W)
            q2 = q_vm[:, pl.ds(at, 2 * W)]
            o2 = do_vm[:, pl.ds(at, 2 * W)]
            q2 = jnp.concatenate([q2[:, :W], q2[:, W:]], axis=0)
            o2 = jnp.concatenate([o2[:, :W], o2[:, W:]], axis=0)
            t = []
            m = None
            for d in range(NSLOT):
                bd = bias[d * W:(d + 1) * W]
                td = dot(keys[d], q2, 1, 1) * (SCALE * LOG2E) + jnp.concatenate([bd, bd], axis=1)
                t.append(td)
                md = jnp.max(td, axis=0, keepdims=True)
                m = md if m is None else jnp.maximum(m, md)
            total = None
            for d in range(NSLOT):
                t[d] = jnp.exp2(t[d] - m)
                ld = jnp.sum(t[d], axis=0, keepdims=True)
                total = ld if total is None else total + ld
            inv = 1.0 / total
            delta = None
            dps = []
            out = pl.ds(pl.multiple_of(p * 2 * W, 2 * W), 2 * W)
            for d in range(NSLOT):
                low = (t[d] * inv).astype(BF)
                pl_vm[d * W:(d + 1) * W, out] = low
                dp = dot(values[d], o2, 1, 1)
                dps.append(dp)
                dd = jnp.sum(low.astype(F32) * dp, axis=0, keepdims=True)
                delta = dd if delta is None else delta + dd
            inv = inv * SCALE
            for d in range(NSLOT):
                ds_vm[d * W:(d + 1) * W, out] = (t[d] * inv * (dps[d] - delta)).astype(BF)
            return c

        lax.fori_loop(0, REP // 2, pair, 0)

        k_all = keys[...].reshape(NSLOT * W, W)
        k_t = k_all.T
        qs = jnp.concatenate(
            [q_vm[:, pl.ds(pl.multiple_of((g * REP + h) * W, W), W)] for h in range(REP)], axis=0
        )
        dos = jnp.concatenate(
            [do_vm[:, pl.ds(pl.multiple_of((g * REP + h) * W, W), W)] for h in range(REP)], axis=0
        )
        for d in range(NSLOT):
            dk = dot(ds_vm[d * W:(d + 1) * W], qs, 1, 0)
            dv = dot(pl_vm[d * W:(d + 1) * W], dos, 1, 0)
            if d == 0:
                own[g, 0] = dk
                own[g, 1] = dv
            else:
                tx[g, 0, d - 1] = dk.astype(BF)
                tx[g, 1, d - 1] = dv.astype(BF)
        for h in range(REP):
            dqt = dot(k_t, ds_vm[:, h * W:(h + 1) * W], 1, 0)
            dq_vm[:, pl.ds(pl.multiple_of((g * REP + h) * W, W), W)] = dqt.T.astype(BF)

    def part_copy(b, d):
        hs = pl.ds(b * GB, GB)
        return remote(
            tx.at[hs, :, d - 1], rx.at[hs, :, d - 1], p_ss.at[b, d], p_rs.at[b, d], (s, j - d)
        )

    def x_peer(e):
        return (sec + e % 2) % 2, (xh + e // 2) % 2

    def gather_one(b, e, along_x):
        mine = dvall.at[b, sec, y, xh]
        if along_x:
            sec2, xh2 = x_peer(e)
            to = dev(sec2, 2 * y + xh2)
        else:
            to = dev(sec, 2 * ((y + e) % 4) + xh)
        return remote(mine, mine, x1_ss.at[b, e], x1_rs.at[b, e], to)

    def gather_two(b, e, along_x):
        if along_x:
            held = dvall.at[b, :, y]
            to = dev(sec, 2 * ((y + e) % 4) + xh)
        else:
            held = dvall.at[b, sec, :, xh]
            sec2, xh2 = x_peer(e)
            to = dev(sec2, 2 * y + xh2)
        return remote(held, held, x2_ss.at[b, e], x2_rs.at[b, e], to)

    def both(b, act):
        @pl.when(b % 2 == 0)
        def _():
            act(True)

        @pl.when(b % 2 == 1)
        def _():
            act(False)

    def reduce(b):
        for d in range(1, NSLOT):
            @pl.when(j + d < 8)
            def _():
                part_copy(b, d).wait_recv()
                for gg in range(GB):
                    g = b * GB + gg
                    own[g] = own[g] + rx[g, :, d - 1].astype(F32)
        for gg in range(GB):
            g = b * GB + gg
            dk_vm[:, pl.ds(pl.multiple_of(g * W, W), W)] = own[g, 0].astype(BF)
            dvall[b, sec, y, xh, :, gg * W:(gg + 1) * W] = own[g, 1].astype(BF)

        def act(along_x):
            for e in range(1, 4):
                gather_one(b, e, along_x).start()

        both(b, act)

    def forward(b):
        def act(along_x):
            for e in range(1, 4):
                gather_one(b, e, along_x).wait_recv()
            for e in range(1, 4):
                gather_two(b, e, along_x).start()

        both(b, act)

    def out_copies(b, act):
        for hh in range(GB):
            for sec2 in range(2):
                target = sec2 * 8 + b * GB + hh
                src = wout.at[b, hh]
                dst = wg_hbm.at[pl.ds(pl.multiple_of(me * ROWS, ROWS), ROWS)]

                @pl.when(target != me)
                def _():
                    act(remote(
                        src, dst, o_ss.at[b, hh * 2 + sec2], o_rs.at[me], dev(sec2, b * GB + hh)
                    ), None)

                @pl.when(target == me)
                def _():
                    act(None, pltpu.make_async_copy(src, dst, out_sem.at[2]))

    def start_out(far, near):
        (far if near is None else near).start()

    def end_out(far, near):
        if near is None:
            far.wait_send()
        else:
            near.wait()

    def weights(b):
        def act(along_x):
            for e in range(1, 4):
                gather_two(b, e, along_x).wait_recv()

        both(b, act)

        @pl.when(b == 0)
        def _():
            l_own.wait()

            def wait_l(k, c):
                l_copy(k).wait_recv()
                return c

            lax.fori_loop(1, 16, wait_l, 0)

        dv = dvall[b].reshape(16 * W, GB * W)
        la = lall[...].reshape(16 * W, ROWS)
        res = dot(la, dv, 0, 0)
        for hh in range(GB):
            wout[b, hh] = res[:, hh * W:(hh + 1) * W].astype(BF)
        out_copies(b, start_out)

    def step(i, c):
        @pl.when(i < NB)
        def _():
            for d in range(1, NSLOT):
                @pl.when(j >= d)
                def _():
                    kv_copy(i, d).wait_recv()

            def group(gg, c2):
                attention(i, i * GB + gg)
                return c2

            lax.fori_loop(0, GB, group, 0)
            for d in range(1, NSLOT):
                @pl.when(j >= d)
                def _():
                    part_copy(i, d).start()

        @pl.when((i >= 1) & (i < NB + 1))
        def _():
            reduce(i - 1)

        @pl.when((i >= 2) & (i < NB + 2))
        def _():
            forward(i - 2)

        @pl.when(i >= 3)
        def _():
            weights(i - 3)

        return c

    lax.fori_loop(0, NB + 3, step, 0)

    dq_out = pltpu.make_async_copy(dq_vm, dq_hbm, out_sem.at[0])
    dk_out = pltpu.make_async_copy(dk_vm, dk_hbm, out_sem.at[1])
    dq_out.start()
    dk_out.start()

    def end_batch(b, c):
        for d in range(1, NSLOT):
            @pl.when(j + d < 8)
            def _():
                kv_copy(b, d).wait_send()

            @pl.when(j >= d)
            def _():
                part_copy(b, d).wait_send()

        def act(along_x):
            for e in range(1, 4):
                gather_one(b, e, along_x).wait_send()
                gather_two(b, e, along_x).wait_send()

        both(b, act)
        out_copies(b, end_out)
        return c

    lax.fori_loop(0, NB, end_batch, 0)
    for d in range(1, NSLOT):
        @pl.when(j + d < 8)
        def _():
            doc_copy(d).wait_send()

    def end_l(k, c):
        l_copy(k).wait_send()
        r = (me + k) % 16
        remote(
            wout.at[0, 0], wg_hbm.at[pl.ds(pl.multiple_of(r * ROWS, ROWS), ROWS)],
            o_ss.at[0, 0], o_rs.at[r], dev(r // 8, r % 8),
        ).wait_recv()
        return c

    lax.fori_loop(1, 16, end_l, 0)
    dq_out.wait()
    dk_out.wait()


def local(queries, key_states, section_value_states, out_grad, layer_input, doc_segments):
    hbm = pl.BlockSpec(memory_space=pl.ANY)
    vmem = pl.BlockSpec(memory_space=pltpu.VMEM)
    dma = pltpu.SemaphoreType.DMA
    dq, dk, wg = pl.pallas_call(
        kernel,
        out_shape=(
            jax.ShapeDtypeStruct((W, 8192), BF),
            jax.ShapeDtypeStruct((W, G * W), BF),
            jax.ShapeDtypeStruct((8192, W), BF),
        ),
        in_specs=[hbm, vmem, vmem, hbm, hbm, vmem],
        out_specs=(hbm, hbm, hbm),
        scratch_shapes=[
            pltpu.VMEM((W, 8192), BF),
            pltpu.VMEM((W, 8192), BF),
            pltpu.VMEM((G, 2, NSLOT, W, W), BF),
            pltpu.VMEM((NSLOT, 8, W), jnp.int32),
            pltpu.VMEM((NSLOT * W, W), F32),
            pltpu.VMEM((G, 2, NSLOT - 1, W, W), BF),
            pltpu.VMEM((G, 2, NSLOT - 1, W, W), BF),
            pltpu.VMEM((G, 2, W, W), F32),
            pltpu.VMEM((NB, 2, 4, 2, W, GB * W), BF),
            pltpu.VMEM((2, 8, W, ROWS), BF),
            pltpu.VMEM((NB, GB, ROWS, W), BF),
            pltpu.VMEM((W, 8192), BF),
            pltpu.VMEM((W, G * W), BF),
            pltpu.VMEM((NSLOT * W, REP * W), BF),
            pltpu.VMEM((NSLOT * W, REP * W), BF),
            dma((3,)),
            dma((NB, NSLOT)), dma((NB, NSLOT)),
            dma((NSLOT,)), dma((NSLOT,)),
            dma((16,)), dma((16,)),
            dma((NB, NSLOT)), dma((NB, NSLOT)),
            dma((NB, 4)), dma((NB, 4)),
            dma((NB, 4)), dma((NB, 4)),
            dma((NB, 4)), dma((16,)),
            dma((3,)),
        ],
        compiler_params=pltpu.CompilerParams(
            collective_id=0, has_side_effects=True, vmem_limit_bytes=56 << 20
        ),
        cost_estimate=pl.CostEstimate(
            flops=10_000_000_000, bytes_accessed=12_000_000, transcendentals=5_000_000
        ),
        name="attention_weight_grad",
    )(
        queries[0], key_states[0], section_value_states[0], out_grad[0], layer_input[0],
        doc_segments,
    )
    return dq[None], dk[None], wg[None]


def solution(mesh):
    rows = P("section", "seq", None)
    return jax.shard_map(
        local,
        mesh=mesh,
        in_specs=(rows, rows, rows, rows, rows, P("section", "seq")),
        out_specs=(rows, rows, P("section", None, "seq")),
        check_vma=False,
    )
```

time: 419 us -> 186 us (0.44)
  Pallas kernels: 0 us -> 178 us
  waiting for transfers between devices: 156 us -> 0 us
  matrix products: 104 us -> 0 us
  starting transfers between devices: 58 us -> 0 us
  local copies, waits for them, and re-layouts: 38.6 us -> 5.28 us
  other arithmetic: 26.2 us -> 0 us
  blocking collectives: 19.7 us -> 0 us
  between operations: 14.2 us -> 0.66 us
    pallas_call x0 -> x1, Pallas kernels: none -> 178 us  [local(): pl.pallas_call(kernel, out_shape=(jax.ShapeDtypeStruct((W, 8192), BF), ja...]
    all_to_all x8 -> x0, waiting for transfers between devices: 155 us -> none  [the longest x1 50.4 us: local(): lax.all_to_all(pieces, 'section', split_axis=0, concat_axis=0, tiled=True)]
    dot_general x49 -> x0, matrix products: 104 us -> none  [the longest x8 27.2 us: one_head(): dprobs = jnp.dot(grad_one, value_col.T, preferred_element_type=jnp.float32)]
    all_to_all x8 -> x0, starting transfers between devices: 58 us -> none  [the longest x1 14 us: local(): lax.all_to_all(pieces, 'section', split_axis=0, concat_axis=0, tiled=True)]
    all_gather x1 -> x0, blocking collectives: 19.7 us -> none  [local(): doc_ids = lax.all_gather(doc_segments[0], 'seq', axis=0, tiled=True)]
    all_to_all x8 -> x0, local copies, waits for them, and re-layouts: 15.2 us -> none  [the longest x2 4.65 us: local(): lax.all_to_all(query_out, 'seq', split_axis=0, concat_axis=1, tiled=True)]
    reduce_sum x16 -> x0, other arithmetic: 14.3 us -> none  [the longest x8 9.32 us: one_head(): jnp.sum(grad_one.astype(jnp.float32) * attended.astype(jnp.float32), axis...]
    convert_element_type x10 -> x0, other arithmetic: 11.9 us -> none  [the longest x8 5.61 us: one_head(): probs_low = attention.astype(jnp.bfloat16)]
  transfers between devices with their start and end apart: 9 -> 0, of which waited for: 6 -> 0; matrix products, arithmetic and copies ran while one was open for 38% -> 0% of each run, Pallas kernels for 0% -> 0%
where the time goes in v1:
time: 186 us; the launch traced here: 184 us
  Pallas kernels  178 us (96%)
  local copies, waits for them, and re-layouts  5.28 us (3%)
    pallas_call x1, Pallas kernels, local(): pl.pallas_call(kernel, out_shape=(jax.ShapeDtypeStruct((W, 8192), BF), ja...  178 us
    unnamed x7, local copies, waits for them, and re-layouts  5.28 us

profile of v1, /device:TPU:1, one launch (start us, length us, event | category | flops | bytes accessed | tf_op | source)
XLA Modules:
  0.0 184.0 jit_solution(9257178555033872956)
XLA Ops:
  0.6 178.1 %attention_weight_grad.1 = (bf16[128,8192]{1,0:T(8,128)(2,1)}, bf16[128,1024]{1,0:T(8,128)(2,1)}, bf16[8192,128]{1,0:T(8,128)(2,1)}) custom-call(bf16[128,8192]{1,0:T(8,128)(2,1)} %bitcast.11, bf16[128,1024]{1,0:T(8,128)(2,1)} %bitcast.14, bf16[128,1024]{1,0:T(8,128)(2,1)} %bitcast.15, bf16[128,8192]{1,0:T(8,128)(2,1)} %bitcast.12, ...), custom_call_target="tpu_custom_call" | custom-call | flops 10000000000 | bytes 12000000 | tf_op jit(solution)/shard_map/attention_weight_grad/pallas_call | solution.py:394
  178.7 0.0 copy-start.1
  178.7 0.0 copy-start
  178.8 3.2 %copy.12 = bf16[1,128,8192]{2,1,0:T(8,128)(2,1)} copy(bf16[1,128,8192]{2,1,0:T(8,128)(2,1)} %bitcast.9) | data formatting | bytes 4194304
  182.0 0.0 copy-done.1
  182.0 0.7 copy.13
  182.7 0.0 copy-done
  182.7 1.3 copy.14
Async XLA Ops:
  178.7 3.3 %copy-start.1 = (bf16[128,1024]{1,0:T(8,128)(2,1)S(1)}, bf16[128,1024]{1,0:T(8,128)(2,1)}, u32[]{:S(2)}) copy-start(bf16[128,1024]{1,0:T(8,128)(2,1)} %get-tuple-element.7) | copy-start | bytes 786436
  178.7 4.0 %copy-start = (bf16[8192,128]{1,0:T(8,128)(2,1)S(1)}, bf16[8192,128]{1,0:T(8,128)(2,1)}, u32[]{:S(2)}) copy-start(bf16[8192,128]{1,0:T(8,128)(2,1)} %get-tuple-element.8) | copy-start | bytes 6291460

commit v2 on v1

v2 whole, which is shorter than its diff:
```python
import math

import jax
import jax.numpy as jnp
from jax import lax
from jax.experimental import pallas as pl
from jax.experimental.pallas import tpu as pltpu
from jax.sharding import PartitionSpec as P

MESH = pl.DeviceIdType.MESH
W = 128
G = 8
REP = 8
NSLOT = 5
NB = 4
GB = G // NB
ROWS = 1024
SCALE = 1.0 / math.sqrt(W)
LOG2E = 1.4426950408889634
BF = jnp.bfloat16
F32 = jnp.float32


def dot(a, b, ca, cb):
    return lax.dot_general(a, b, (((ca,), (cb,)), ((), ())), preferred_element_type=F32)


def kernel(
    q_hbm, k_ref, v_ref, do_hbm, l_hbm, doc_ref,
    dq_hbm, dk_hbm, wg_hbm,
    q_vm, do_vm, kv, docx, bias, prob, low_vm, ds_vm, acc, xtx, xrx, ytx, yrx, dvall, lall, lt,
    keep, wtx, wrx, wout, dq_vm, dk_vm,
    in_sem, doc_ss, doc_rs, ky_ss, ky_rs, kx_ss, kx_rs, l_ss, l_rs, px_ss, px_rs, py_ss, py_rs,
    gx_ss, gx_rs, gy_ss, gy_rs, w_ss, w_rs, o_ss, o_rs, out_sem,
):
    s = lax.axis_index("section")
    j = lax.axis_index("seq")
    sec = s // 8
    y = j // 2
    xh = j % 2
    mine = ((sec + xh) % 2) * 4 + y
    partner = j + 1 - 2 * xh

    def remote(src, dst, ss, rs, to):
        return pltpu.make_async_remote_copy(
            src_ref=src, dst_ref=dst, send_sem=ss, recv_sem=rs, device_id=to, device_id_type=MESH
        )

    def of_section(sec2):
        return s + (sec2 + sec - 2 * sec * sec2) * (15 - 2 * s)

    def holder(r):
        return of_section((r // 4 + xh) % 2), 2 * (r % 4) + xh

    def rows_of(r):
        return pl.ds(pl.multiple_of(r * ROWS, ROWS), ROWS)

    def heads(b):
        return pl.ds(b * GB, GB)

    q_in = pltpu.make_async_copy(q_hbm, q_vm, in_sem.at[0])
    do_in = pltpu.make_async_copy(do_hbm, do_vm, in_sem.at[1])
    l_own = pltpu.make_async_copy(l_hbm.at[:, rows_of(mine)], lall.at[sec, y], in_sem.at[2])
    q_in.start()
    do_in.start()
    l_own.start()

    barrier = pltpu.get_barrier_semaphore()

    def greet(to):
        pl.semaphore_signal(barrier, inc=1, device_id=to, device_id_type=MESH)

    def greet_own(k, c):
        greet((s, (j + k) % 8))
        return c

    def greet_mirror(k, c):
        greet((15 - s, 2 * k + xh))
        return c

    lax.fori_loop(1, 8, greet_own, 0)
    lax.fori_loop(0, 4, greet_mirror, 0)
    greet((15 - s, partner))

    for g in range(G):
        kv[0, g, 0] = k_ref[:, g * W:(g + 1) * W]
        kv[1, g, 0] = v_ref[:, g * W:(g + 1) * W]
    docx[0] = jnp.broadcast_to(doc_ref[...], (8, W))
    for d in range(1, NSLOT):
        @pl.when(j < d)
        def _():
            kv[:, :, d] = jnp.zeros((2, G, W, W), BF)
            docx[d] = jnp.zeros((8, W), jnp.int32)

    pl.semaphore_wait(barrier, 12)

    def doc_copy(d):
        return remote(docx.at[0], docx.at[d], doc_ss.at[d], doc_rs.at[d], (s, j + d))

    def kv_y(kind, b, n):
        return remote(
            kv.at[kind, heads(b), 0], kv.at[kind, heads(b), 2 * n + 2],
            ky_ss.at[kind, b, n], ky_rs.at[kind, b, n], (s, j + 2 * n + 2),
        )

    def kv_x(kind, b, n):
        return remote(
            kv.at[kind, heads(b), 2 * n + 2 * xh], kv.at[kind, heads(b), 2 * n + 1],
            kx_ss.at[kind, b, n], kx_rs.at[kind, b, n], (s, partner),
        )

    def send_kv(kind, b):
        @pl.when(xh == 0)
        def _():
            kv_x(kind, b, 0).start()

        for n in range(2):
            @pl.when(j + 2 * n + 2 < 8)
            def _():
                kv_y(kind, b, n).start()

    def relay_kv(kind, b):
        for n in range(2):
            @pl.when(j >= 2 * n + 2)
            def _():
                kv_y(kind, b, n).wait_recv()

        for n in range(2):
            @pl.when((j >= 2 * n + 2 * xh) & (n + xh > 0))
            def _():
                kv_x(kind, b, n).start()

    def got_kv(kind, b):
        for n in range(2):
            @pl.when(j >= 2 * n + 1)
            def _():
                kv_x(kind, b, n).wait_recv()

    for d in range(1, NSLOT):
        @pl.when(j + d < 8)
        def _():
            doc_copy(d).start()

    def send_all(b, c):
        send_kv(0, b)
        return c

    lax.fori_loop(0, NB, send_all, 0)

    def send_v(b, c):
        send_kv(1, b)
        return c

    lax.fori_loop(0, NB, send_v, 0)

    def l_copy(k):
        r = (mine + k) % 8
        return remote(l_hbm.at[:, rows_of(r)], lall.at[sec, y], l_ss.at[k], l_rs.at[k], holder(r))

    def send_l(k, c):
        l_copy(k).start()
        return c

    lax.fori_loop(1, 8, send_l, 0)

    for d in range(1, NSLOT):
        @pl.when(j >= d)
        def _():
            doc_copy(d).wait_recv()

    row = lax.broadcasted_iota(jnp.int32, (W, W), 0)
    col = lax.broadcasted_iota(jnp.int32, (W, W), 1)
    q_doc = jnp.broadcast_to(docx[0, 0:1], (W, W)).astype(F32)
    for d in range(NSLOT):
        key_doc = jnp.broadcast_to(docx[d, 0:1], (W, W)).astype(F32).T
        seen = (key_doc == q_doc) & (j >= d)
        if d == 0:
            seen = seen & (row <= col)
        bias[d * W:(d + 1) * W] = jnp.where(seen, 0.0, -jnp.inf).astype(F32)

    q_in.wait()
    do_in.wait()

    def two_heads(ref, g, p):
        both = ref[:, pl.ds(pl.multiple_of((g * REP + 2 * p) * W, 2 * W), 2 * W)]
        return jnp.concatenate([both[:, :W], both[:, W:]], axis=0)

    def group_rows(ref, g):
        return jnp.concatenate(
            [ref[:, pl.ds(pl.multiple_of((g * REP + h) * W, W), W)] for h in range(REP)], axis=0
        )

    def part_sums(kind, g, left, right):
        for d in range(NSLOT):
            part = dot(left[d * W:(d + 1) * W], right, 1, 0)
            if d % 2 == 0:
                acc[kind, g, d // 2] = part
            else:
                xtx[kind, g, d // 2] = part.astype(BF)

    def probabilities(g):
        keys = kv.at[0, g]

        def pair(p, c):
            q2 = two_heads(q_vm, g, p)
            t = []
            m = None
            for d in range(NSLOT):
                bd = bias[d * W:(d + 1) * W]
                td = dot(keys[d], q2, 1, 1) * (SCALE * LOG2E) + jnp.concatenate([bd, bd], axis=1)
                t.append(td)
                md = jnp.max(td, axis=0, keepdims=True)
                m = md if m is None else jnp.maximum(m, md)
            total = None
            for d in range(NSLOT):
                t[d] = jnp.exp2(t[d] - m)
                ld = jnp.sum(t[d], axis=0, keepdims=True)
                total = ld if total is None else total + ld
            inv = 1.0 / total
            out = pl.ds(pl.multiple_of(p * 2 * W, 2 * W), 2 * W)
            for d in range(NSLOT):
                pd = t[d] * inv
                prob[g, p, d * W:(d + 1) * W] = pd
                low_vm[d * W:(d + 1) * W, out] = pd.astype(BF)
            return c

        lax.fori_loop(0, REP // 2, pair, 0)
        part_sums(1, g, low_vm, group_rows(do_vm, g))

    def score_grads(g):
        values = kv.at[1, g]

        def pair(p, c):
            o2 = two_heads(do_vm, g, p)
            delta = None
            dps = []
            for d in range(NSLOT):
                dp = dot(values[d], o2, 1, 1)
                dps.append(dp)
                low = prob[g, p, d * W:(d + 1) * W].astype(BF).astype(F32)
                dd = jnp.sum(low * dp, axis=0, keepdims=True)
                delta = dd if delta is None else delta + dd
            out = pl.ds(pl.multiple_of(p * 2 * W, 2 * W), 2 * W)
            for d in range(NSLOT):
                pd = prob[g, p, d * W:(d + 1) * W]
                ds_vm[d * W:(d + 1) * W, out] = (pd * ((dps[d] - delta) * SCALE)).astype(BF)
            return c

        lax.fori_loop(0, REP // 2, pair, 0)
        part_sums(0, g, ds_vm, group_rows(q_vm, g))
        k_t = kv[0, g].reshape(NSLOT * W, W).T
        for h in range(REP):
            dqt = dot(k_t, ds_vm[:, h * W:(h + 1) * W], 1, 0)
            dq_vm[:, pl.ds(pl.multiple_of((g * REP + h) * W, W), W)] = dqt.T.astype(BF)

    def part_x(kind, b, n):
        return remote(
            xtx.at[kind, heads(b), n], xrx.at[kind, heads(b), n],
            px_ss.at[kind, b, n], px_rs.at[kind, b, n], (s, partner),
        )

    def part_y(kind, b, n):
        return remote(
            ytx.at[kind, heads(b), n], yrx.at[kind, heads(b), n],
            py_ss.at[kind, b, n], py_rs.at[kind, b, n], (s, j - 2 * n - 2),
        )

    def send_parts(kind, b):
        for n in range(2):
            @pl.when(j >= 2 * n + 1)
            def _():
                part_x(kind, b, n).start()

    def cross_parts(kind, b):
        for n in range(2):
            @pl.when(partner >= 2 * n + 1)
            def _():
                part_x(kind, b, n).wait_recv()
                for gg in range(GB):
                    g = b * GB + gg
                    acc[kind, g, n + xh] = acc[kind, g, n + xh] + xrx[kind, g, n].astype(F32)

        for n in range(2):
            @pl.when(j >= 2 * n + 2)
            def _():
                ytx[kind, heads(b), n] = acc[kind, heads(b), n + 1].astype(BF)
                part_y(kind, b, n).start()

    def own_sums(kind, b):
        for n in range(2):
            @pl.when(j + 2 * n + 2 < 8)
            def _():
                part_y(kind, b, n).wait_recv()
                for gg in range(GB):
                    g = b * GB + gg
                    acc[kind, g, 0] = acc[kind, g, 0] + yrx[kind, g, n].astype(F32)

    def gather_x(b):
        block = dvall.at[b, sec, y]
        return remote(block, block, gx_ss.at[b], gx_rs.at[b], (15 - s, j))

    def gather_y(b, e):
        blocks = dvall.at[b, :, y]
        to = (s, 2 * ((y + e) % 4) + xh)
        return remote(blocks, blocks, gy_ss.at[b, e], gy_rs.at[b, e], to)

    def value_grads(b):
        own_sums(1, b)
        for gg in range(GB):
            dvall[b, sec, y, :, gg * W:(gg + 1) * W] = acc[1, b * GB + gg, 0].astype(BF)
        gather_x(b).start()

    def key_grads(b):
        own_sums(0, b)
        for gg in range(GB):
            g = b * GB + gg
            dk_vm[:, pl.ds(pl.multiple_of(g * W, W), W)] = acc[0, g, 0].astype(BF)

    def forward(b):
        gather_x(b).wait_recv()
        for e in range(1, 4):
            gather_y(b, e).start()

    def w_copy(b):
        return remote(wtx.at[b], wrx.at[b], w_ss.at[b], w_rs.at[b], (15 - s, partner))

    def weights(b):
        for e in range(1, 4):
            gather_y(b, e).wait_recv()

        @pl.when(b == 0)
        def _():
            l_own.wait()

            def wait_l(k, c):
                l_copy(k).wait_recv()
                return c

            lax.fori_loop(1, 8, wait_l, 0)
            for r in range(ROWS // W):
                la = lall[:, :, :, r * W:(r + 1) * W].reshape(8 * W, W)
                lt[r * W:(r + 1) * W] = la.T

        dv = dvall[b].reshape(8 * W, GB * W)

        def chunk(r, c):
            at = pl.ds(pl.multiple_of(r * 2 * W, 2 * W), 2 * W)
            res = dot(lt[at], dv, 1, 0)
            keep[b, at] = jnp.where(xh == 0, res[:, :W], res[:, W:])
            wtx[b, at] = jnp.where(xh == 0, res[:, W:], res[:, :W]).astype(BF)
            return c

        lax.fori_loop(0, ROWS // (2 * W), chunk, 0)
        w_copy(b).start()

    def out_copies(b, far, near):
        for sec2 in range(2):
            at_home = (sec2 == sec) & (b == y)
            src, dst = wout.at[b], wg_hbm.at[rows_of(mine)]

            @pl.when(jnp.logical_not(at_home))
            def _():
                far(remote(
                    src, dst, o_ss.at[b, sec2], o_rs.at[mine], (of_section(sec2), 2 * b + xh)
                ))

            @pl.when(at_home)
            def _():
                near(pltpu.make_async_copy(src, dst, out_sem.at[2]))

    def finish(b):
        w_copy(b).wait_recv()
        wout[b] = (keep[b] + wrx[b].astype(F32)).astype(BF)
        out_copies(b, lambda c: c.start(), lambda c: c.start())

    relay_kv(0, 0)

    def step(i, c):
        def at(first, do, *args):
            @pl.when((i >= first) & (i < first + NB))
            def _():
                do(*args, i - first)

        @pl.when(i < NB - 1)
        def _():
            relay_kv(0, i + 1)

        @pl.when((i >= NB - 1) & (i < 2 * NB - 1))
        def _():
            relay_kv(1, i - (NB - 1))

        def first_half(b):
            got_kv(0, b)

            def group(gg, c2):
                probabilities(b * GB + gg)
                return c2

            lax.fori_loop(0, GB, group, 0)
            send_parts(1, b)

        def second_half(b):
            got_kv(1, b)

            def group(gg, c2):
                score_grads(b * GB + gg)
                return c2

            lax.fori_loop(0, GB, group, 0)
            send_parts(0, b)

        at(0, first_half)
        at(1, cross_parts, 1)
        at(2, value_grads)
        at(3, forward)
        at(4, weights)
        at(5, finish)
        at(NB, second_half)
        at(NB + 1, cross_parts, 0)
        at(NB + 2, key_grads)
        return c

    lax.fori_loop(0, 2 * NB + 2, step, 0)

    dq_out = pltpu.make_async_copy(dq_vm, dq_hbm, out_sem.at[0])
    dk_out = pltpu.make_async_copy(dk_vm, dk_hbm, out_sem.at[1])
    dq_out.start()
    dk_out.start()

    def end_batch(b, c):
        for kind in range(2):
            @pl.when(xh == 0)
            def _():
                kv_x(kind, b, 0).wait_send()

            for n in range(2):
                @pl.when(j + 2 * n + 2 < 8)
                def _():
                    kv_y(kind, b, n).wait_send()

                @pl.when((j >= 2 * n + 2 * xh) & (n + xh > 0))
                def _():
                    kv_x(kind, b, n).wait_send()

                @pl.when(j >= 2 * n + 1)
                def _():
                    part_x(kind, b, n).wait_send()

                @pl.when(j >= 2 * n + 2)
                def _():
                    part_y(kind, b, n).wait_send()

        gather_x(b).wait_send()
        for e in range(1, 4):
            gather_y(b, e).wait_send()
        w_copy(b).wait_send()
        out_copies(b, lambda c: c.wait_send(), lambda c: c.wait())
        return c

    lax.fori_loop(0, NB, end_batch, 0)
    for d in range(1, NSLOT):
        @pl.when(j + d < 8)
        def _():
            doc_copy(d).wait_send()

    def end_l(k, c):
        l_copy(k).wait_send()
        r = (mine + k) % 8
        remote(
            wout.at[0], wg_hbm.at[rows_of(r)], o_ss.at[0, 0], o_rs.at[r], holder(r)
        ).wait_recv()
        return c

    lax.fori_loop(1, 8, end_l, 0)
    dq_out.wait()
    dk_out.wait()


def local(queries, key_states, section_value_states, out_grad, layer_input, doc_segments):
    hbm = pl.BlockSpec(memory_space=pl.ANY)
    vmem = pl.BlockSpec(memory_space=pltpu.VMEM)
    dma = pltpu.SemaphoreType.DMA
    dq, dk, wg = pl.pallas_call(
        kernel,
        out_shape=(
            jax.ShapeDtypeStruct((W, 8192), BF),
            jax.ShapeDtypeStruct((W, G * W), BF),
            jax.ShapeDtypeStruct((8192, W), BF),
        ),
        in_specs=[hbm, vmem, vmem, hbm, hbm, vmem],
        out_specs=(hbm, hbm, hbm),
        scratch_shapes=[
            pltpu.VMEM((W, 8192), BF),
            pltpu.VMEM((W, 8192), BF),
            pltpu.VMEM((2, G, NSLOT, W, W), BF),
            pltpu.VMEM((NSLOT, 8, W), jnp.int32),
            pltpu.VMEM((NSLOT * W, W), F32),
            pltpu.VMEM((G, REP // 2, NSLOT * W, 2 * W), F32),
            pltpu.VMEM((NSLOT * W, REP * W), BF),
            pltpu.VMEM((NSLOT * W, REP * W), BF),
            pltpu.VMEM((2, G, 3, W, W), F32),
            pltpu.VMEM((2, G, 2, W, W), BF),
            pltpu.VMEM((2, G, 2, W, W), BF),
            pltpu.VMEM((2, G, 2, W, W), BF),
            pltpu.VMEM((2, G, 2, W, W), BF),
            pltpu.VMEM((NB, 2, 4, W, GB * W), BF),
            pltpu.VMEM((2, 4, W, ROWS), BF),
            pltpu.VMEM((ROWS, 8 * W), BF),
            pltpu.VMEM((NB, ROWS, W), F32),
            pltpu.VMEM((NB, ROWS, W), BF),
            pltpu.VMEM((NB, ROWS, W), BF),
            pltpu.VMEM((NB, ROWS, W), BF),
            pltpu.VMEM((W, 8192), BF),
            pltpu.VMEM((W, G * W), BF),
            dma((3,)),
            dma((NSLOT,)), dma((NSLOT,)),
            dma((2, NB, 2)), dma((2, NB, 2)),
            dma((2, NB, 2)), dma((2, NB, 2)),
            dma((8,)), dma((8,)),
            dma((2, NB, 2)), dma((2, NB, 2)),
            dma((2, NB, 2)), dma((2, NB, 2)),
            dma((NB,)), dma((NB,)),
            dma((NB, 4)), dma((NB, 4)),
            dma((NB,)), dma((NB,)),
            dma((NB, 2)), dma((8,)),
            dma((3,)),
        ],
        compiler_params=pltpu.CompilerParams(
            collective_id=0, has_side_effects=True, vmem_limit_bytes=58 << 20
        ),
        cost_estimate=pl.CostEstimate(
            flops=10_000_000_000, bytes_accessed=12_000_000, transcendentals=5_000_000
        ),
        name="attention_weight_grad",
    )(
        queries[0], key_states[0], section_value_states[0], out_grad[0], layer_input[0],
        doc_segments,
    )
    return dq[None], dk[None], wg[None]


def solution(mesh):
    rows = P("section", "seq", None)
    return jax.shard_map(
        local,
        mesh=mesh,
        in_specs=(rows, rows, rows, rows, rows, P("section", "seq")),
        out_specs=(rows, rows, P("section", None, "seq")),
        check_vma=False,
    )
```

time: 186 us -> 194 us (1.043)
  the two profiles are of different devices: /device:TPU:1 before, /device:TPU:30 now
where the time goes in v2:
time: 194 us; the launch traced here: 193 us
  Pallas kernels  188 us (97%)
  local copies, waits for them, and re-layouts  5.28 us (3%)
    pallas_call x1, Pallas kernels, local(): pl.pallas_call(kernel, out_shape=(jax.ShapeDtypeStruct((W, 8192), BF), ja...  188 us
    unnamed x7, local copies, waits for them, and re-layouts  5.28 us

profile of v2, /device:TPU:30, one launch (start us, length us, event | category | flops | bytes accessed | tf_op | source)
XLA Modules:
  0.0 193.4 jit_solution(2797816126546657227)
XLA Ops:
  0.6 187.5 %attention_weight_grad.1 = (bf16[128,8192]{1,0:T(8,128)(2,1)}, bf16[128,1024]{1,0:T(8,128)(2,1)}, bf16[8192,128]{1,0:T(8,128)(2,1)}) custom-call(bf16[128,8192]{1,0:T(8,128)(2,1)} %bitcast.11, bf16[128,1024]{1,0:T(8,128)(2,1)} %bitcast.14, bf16[128,1024]{1,0:T(8,128)(2,1)} %bitcast.15, bf16[128,8192]{1,0:T(8,128)(2,1)} %bitcast.12, ...), custom_call_target="tpu_custom_call" | custom-call | flops 10000000000 | bytes 12000000 | tf_op jit(solution)/shard_map/attention_weight_grad/pallas_call | solution.py:483
  188.1 0.0 copy-start.1
  188.2 0.0 copy-start
  188.2 3.2 %copy.12 = bf16[1,128,8192]{2,1,0:T(8,128)(2,1)} copy(bf16[1,128,8192]{2,1,0:T(8,128)(2,1)} %bitcast.9) | data formatting | bytes 4194304
  191.4 0.0 copy-done.1
  191.4 0.7 copy.13
  192.1 0.0 copy-done
  192.1 1.3 copy.14
Async XLA Ops:
  188.1 3.3 %copy-start.1 = (bf16[128,1024]{1,0:T(8,128)(2,1)S(1)}, bf16[128,1024]{1,0:T(8,128)(2,1)}, u32[]{:S(2)}) copy-start(bf16[128,1024]{1,0:T(8,128)(2,1)} %get-tuple-element.7) | copy-start | bytes 786436
  188.2 4.0 %copy-start = (bf16[8192,128]{1,0:T(8,128)(2,1)S(1)}, bf16[8192,128]{1,0:T(8,128)(2,1)}, u32[]{:S(2)}) copy-start(bf16[8192,128]{1,0:T(8,128)(2,1)} %get-tuple-element.8) | copy-start | bytes 6291460

commit v3 on v2

--- a/solution.py
+++ b/solution.py
@@ -31,7 +31,7 @@
     q_vm, do_vm, kv, docx, bias, prob, low_vm, ds_vm, acc, xtx, xrx, ytx, yrx, dvall, lall, lt,
     keep, wtx, wrx, wout, dq_vm, dk_vm,
     in_sem, doc_ss, doc_rs, ky_ss, ky_rs, kx_ss, kx_rs, l_ss, l_rs, px_ss, px_rs, py_ss, py_rs,
-    gx_ss, gx_rs, gy_ss, gy_rs, w_ss, w_rs, o_ss, o_rs, out_sem,
+    gx_ss, gx_rs, gy_ss, gy_rs, w_ss, w_rs, oy_ss, oy_rs, ox_ss, ox_rs, out_sem,
 ):
     s = lax.axis_index("section")
     j = lax.axis_index("seq")
@@ -147,21 +147,16 @@
 
     lax.fori_loop(0, NB, send_all, 0)
 
-    def send_v(b, c):
-        send_kv(1, b)
-        return c
-
-    lax.fori_loop(0, NB, send_v, 0)
+    def peer(k):
+        return ((sec + k // 4 + xh) % 2) * 4 + (y + k) % 4
 
     def l_copy(k):
-        r = (mine + k) % 8
+        r = peer(k)
         return remote(l_hbm.at[:, rows_of(r)], lall.at[sec, y], l_ss.at[k], l_rs.at[k], holder(r))
 
     def send_l(k, c):
         l_copy(k).start()
         return c
-
-    lax.fori_loop(1, 8, send_l, 0)
 
     for d in range(1, NSLOT):
         @pl.when(j >= d)
@@ -324,16 +319,24 @@
     def w_copy(b):
         return remote(wtx.at[b], wrx.at[b], w_ss.at[b], w_rs.at[b], (15 - s, partner))
 
-    def weights(b):
-        for e in range(1, 4):
-            gather_y(b, e).wait_recv()
-
-        @pl.when(b == 0)
-        def _():
+    def turn(k):
+        return (y + k) % 4
+
+    def weights(k):
+        b = turn(k)
+
+        @pl.when(k == 0)
+        def _():
+            def wait_gather(b2, c):
+                for e in range(1, 4):
+                    gather_y(b2, e).wait_recv()
+                return c
+
+            lax.fori_loop(0, NB, wait_gather, 0)
             l_own.wait()
 
-            def wait_l(k, c):
-                l_copy(k).wait_recv()
+            def wait_l(k2, c):
+                l_copy(k2).wait_recv()
                 return c
 
             lax.fori_loop(1, 8, wait_l, 0)
@@ -353,25 +356,46 @@
         lax.fori_loop(0, ROWS // (2 * W), chunk, 0)
         w_copy(b).start()
 
-    def out_copies(b, far, near):
-        for sec2 in range(2):
-            at_home = (sec2 == sec) & (b == y)
-            src, dst = wout.at[b], wg_hbm.at[rows_of(mine)]
-
-            @pl.when(jnp.logical_not(at_home))
-            def _():
-                far(remote(
-                    src, dst, o_ss.at[b, sec2], o_rs.at[mine], (of_section(sec2), 2 * b + xh)
-                ))
-
-            @pl.when(at_home)
-            def _():
-                near(pltpu.make_async_copy(src, dst, out_sem.at[2]))
-
-    def finish(b):
+    def column_rows(y2):
+        return rows_of(((sec + xh) % 2) * 4 + y2)
+
+    def out_y(k):
+        b = turn(k)
+        return remote(
+            wout.at[b], wg_hbm.at[rows_of(mine)], oy_ss.at[k], oy_rs.at[k], (s, 2 * b + xh)
+        )
+
+    def out_own():
+        return pltpu.make_async_copy(wout.at[y], wg_hbm.at[rows_of(mine)], out_sem.at[2])
+
+    def hand_own():
+        return remote(
+            wout.at[y], wg_hbm.at[rows_of(mine)], ox_ss.at[0], ox_rs.at[0], (15 - s, j)
+        )
+
+    def hand_on(k):
+        at = wg_hbm.at[column_rows((y + 4 - k) % 4)]
+        return remote(at, at, ox_ss.at[k], ox_rs.at[k], (15 - s, j))
+
+    def finish(k):
+        b = turn(k)
         w_copy(b).wait_recv()
         wout[b] = (keep[b] + wrx[b].astype(F32)).astype(BF)
-        out_copies(b, lambda c: c.start(), lambda c: c.start())
+
+        @pl.when(k == 0)
+        def _():
+            out_own().start()
+            hand_own().start()
+
+        @pl.when(k > 0)
+        def _():
+            out_y(k).start()
+
+    def pass_on(k):
+        @pl.when(k > 0)
+        def _():
+            out_y(k).wait_recv()
+            hand_on(k).start()
 
     relay_kv(0, 0)
 
@@ -384,6 +408,14 @@
         @pl.when(i < NB - 1)
         def _():
             relay_kv(0, i + 1)
+
+        @pl.when(i < NB)
+        def _():
+            send_kv(1, i)
+
+        @pl.when((i >= 2) & (i < 6))
+        def _():
+            lax.fori_loop(jnp.maximum(2 * i - 4, 1), 2 * i - 2, send_l, 0)
 
         @pl.when((i >= NB - 1) & (i < 2 * NB - 1))
         def _():
@@ -413,14 +445,15 @@
         at(1, cross_parts, 1)
         at(2, value_grads)
         at(3, forward)
-        at(4, weights)
-        at(5, finish)
+        at(7, weights)
+        at(8, finish)
+        at(9, pass_on)
         at(NB, second_half)
         at(NB + 1, cross_parts, 0)
         at(NB + 2, key_grads)
         return c
 
-    lax.fori_loop(0, 2 * NB + 2, step, 0)
+    lax.fori_loop(0, NB + 9, step, 0)
 
     dq_out = pltpu.make_async_copy(dq_vm, dq_hbm, out_sem.at[0])
     dk_out = pltpu.make_async_copy(dk_vm, dk_hbm, out_sem.at[1])
@@ -454,7 +487,6 @@
         for e in range(1, 4):
             gather_y(b, e).wait_send()
         w_copy(b).wait_send()
-        out_copies(b, lambda c: c.wait_send(), lambda c: c.wait())
         return c
 
     lax.fori_loop(0, NB, end_batch, 0)
@@ -465,13 +497,18 @@
 
     def end_l(k, c):
         l_copy(k).wait_send()
-        r = (mine + k) % 8
-        remote(
-            wout.at[0], wg_hbm.at[rows_of(r)], o_ss.at[0, 0], o_rs.at[r], holder(r)
-        ).wait_recv()
         return c
 
     lax.fori_loop(1, 8, end_l, 0)
+    out_own().wait()
+    hand_own().wait()
+
+    def end_out(k, c):
+        out_y(k).wait_send()
+        hand_on(k).wait()
+        return c
+
+    lax.fori_loop(1, 4, end_out, 0)
     dq_out.wait()
     dk_out.wait()
 
@@ -522,7 +559,8 @@
             dma((NB,)), dma((NB,)),
             dma((NB, 4)), dma((NB, 4)),
             dma((NB,)), dma((NB,)),
-            dma((NB, 2)), dma((8,)),
+            dma((4,)), dma((4,)),
+            dma((4,)), dma((4,)),
             dma((3,)),
         ],
         compiler_params=pltpu.CompilerParams(

time: 194 us -> 156 us (0.80)
  the two profiles are of different devices: /device:TPU:30 before, /device:TPU:1 now
where the time goes in v3:
time: 156 us; the launch traced here: 155 us
  Pallas kernels  149 us (96%)
  local copies, waits for them, and re-layouts  5.28 us (3%)
    pallas_call x1, Pallas kernels, local(): pl.pallas_call(kernel, out_shape=(jax.ShapeDtypeStruct((W, 8192), BF), ja...  149 us
    unnamed x7, local copies, waits for them, and re-layouts  5.28 us

profile of v3, /device:TPU:1, one launch (start us, length us, event | category | flops | bytes accessed | tf_op | source)
XLA Modules:
  0.0 154.7 jit_solution(12526486546211032695)
XLA Ops:
  0.6 148.8 %attention_weight_grad.1 = (bf16[128,8192]{1,0:T(8,128)(2,1)}, bf16[128,1024]{1,0:T(8,128)(2,1)}, bf16[8192,128]{1,0:T(8,128)(2,1)}) custom-call(bf16[128,8192]{1,0:T(8,128)(2,1)} %bitcast.11, bf16[128,1024]{1,0:T(8,128)(2,1)} %bitcast.14, bf16[128,1024]{1,0:T(8,128)(2,1)} %bitcast.15, bf16[128,8192]{1,0:T(8,128)(2,1)} %bitcast.12, ...), custom_call_target="tpu_custom_call" | custom-call | flops 10000000000 | bytes 12000000 | tf_op jit(solution)/shard_map/attention_weight_grad/pallas_call | solution.py:520
  149.4 0.0 copy-start.1
  149.4 0.0 copy-start
  149.4 3.2 %copy.12 = bf16[1,128,8192]{2,1,0:T(8,128)(2,1)} copy(bf16[1,128,8192]{2,1,0:T(8,128)(2,1)} %bitcast.9) | data formatting | bytes 4194304
  152.7 0.0 copy-done.1
  152.7 0.7 copy.13
  153.4 0.0 copy-done
  153.4 1.3 copy.14
Async XLA Ops:
  149.4 3.3 %copy-start.1 = (bf16[128,1024]{1,0:T(8,128)(2,1)S(1)}, bf16[128,1024]{1,0:T(8,128)(2,1)}, u32[]{:S(2)}) copy-start(bf16[128,1024]{1,0:T(8,128)(2,1)} %get-tuple-element.7) | copy-start | bytes 786436
  149.4 4.0 %copy-start = (bf16[8192,128]{1,0:T(8,128)(2,1)S(1)}, bf16[8192,128]{1,0:T(8,128)(2,1)}, u32[]{:S(2)}) copy-start(bf16[8192,128]{1,0:T(8,128)(2,1)} %get-tuple-element.8) | copy-start | bytes 6291460
